TPU v7x, 32 devices: a whole 2x2x4 slice. The times are simulated.
32 devices in a mesh: row: 4 (over z), col: 8 (over y, x, core).
Axes of the slice: x: 2, y: 2, z: 4, core: 2. Of those that a mesh axis runs over, the one named last changes fastest.
Arguments:
- tokens: bfloat16 [96, 12288], P('col', 'row'), may hold values from -6 to 6
- up_weight: bfloat16 [12288, 49152], P('row', 'col'), may hold values from -0.0546875 to 0.0546875
- up_bias: float32 [49152], P('col'), may hold values from -3 to 3
- down_weight: bfloat16 [49152, 12288], P('col', 'row'), may hold values from -0.02734375 to 0.02734375
- down_bias: float32 [12288], P('row'), may hold values from -3 to 3
Outputs:
- layer_out: bfloat16 [96, 12288], P('col', 'row')
All inputs are finite; a program needn't handle non-finite values.
Results may differ from a plain program's by a relative error of at most 0.0034.
Values may be sent and summed in bfloat16 or wider, within the bound.
A program may use at most 128 MiB of HBM per device.

v0:
```python
import jax
import jax.numpy as jnp
from jax import lax
from jax.sharding import PartitionSpec as P


def on_device(tokens, up_weight, up_bias, down_weight, down_bias):
    gathered = lax.all_gather(tokens, "col", axis=0, tiled=True)
    partial_up = jnp.dot(gathered, up_weight, preferred_element_type=jnp.float32)
    summed_up = lax.psum(partial_up, "row")
    activated = jax.nn.gelu(summed_up + up_bias, approximate=True).astype(jnp.bfloat16)
    branch = lax.psum_scatter(
        jnp.dot(activated, down_weight, preferred_element_type=jnp.float32),
        "col",
        scatter_dimension=0,
        tiled=True,
    )
    return (tokens.astype(jnp.float32) + branch + down_bias).astype(jnp.bfloat16)


def solution(mesh):
    placed = (P("col", "row"), P("row", "col"), P("col"), P("col", "row"), P("row"))
    return jax.shard_map(
        on_device, mesh=mesh, in_specs=placed, out_specs=P("col", "row"), check_vma=False
    )
```

profile of v0, /device:TPU:1, one launch (start us, length us, event | category | flops | bytes accessed | tf_op | source)
XLA Modules:
  0.0 186.9 jit_solution(4418884062678191413)
XLA Ops:
  6.5 0.0 all-reduce.4.cloned.1.call-start
  6.5 12.1 %all-gather = bf16[8,12,3072]{2,1,0:T(8,128)(2,1)S(1)} all-gather(bf16[1,12,3072]{2,1,0:T(8,128)(2,1)} %bitcast.7), channel_id=1, replica_groups=mesh['row'=4,'col'=8] {'col'}, dimensions={0}, use_global_device_ids=true | all-gather | bytes 663552 | tf_op jit(solution)/shard_map/all_gather | solution.py:8
  18.6 0.1 reshape.3
  18.8 16.3 %fusion.22 = f32[96,6144]{1,0:T(8,128)} fusion(bf16[96,3072]{1,0:T(8,128)(2,1)S(1)} %reshape.3, bf16[3072,6144]{1,0:T(8,128)(2,1)} %param.6), kind=kOutput, calls=%fused_computation.22 | convolution fusion | flops 3623878656 | bytes 40697856 | tf_op jit(solution)/shard_map/dot_general | solution.py:9
  35.0 0.0 copy-start.1
  35.0 0.0 all-reduce.4.cloned.1.call-update
  35.1 0.0 copy-start.3
  35.1 95.5 %all-reduce.4.cloned.1.call-done = f32[96,6144]{1,0:T(8,128)} async-done(((f32[96,6144]{1,0:T(8,128)}), f32[96,6144]{1,0:T(8,128)}) %all-reduce.4.cloned.1.call-update) | async-done | bytes 2359312 | tf_op jit(solution)/shard_map/psum | solution.py:10
  130.6 0.0 copy-done.1
  130.6 15.7 %fusion.9 = f32[96,3072]{1,0:T(8,128)S(1)} fusion(bf16[6144,3072]{1,0:T(8,128)(2,1)} %param.8, f32[96,6144]{1,0:T(8,128)} %all-reduce.4.cloned.1.call-done, f32[6144]{0:T(1024)S(1)} %copy-done.1), kind=kOutput, calls=%fused_computation.9 | convolution fusion | flops 3629776896 | bytes 41312256 | tf_op jit(solution)/shard_map/dot_general | solution.py:13
  146.3 0.0 copy-start
  146.3 0.0 copy-start.2
  146.3 21.6 %fusion = f32[16,3072]{1,0:T(8,128)S(1)} fusion(f32[96,3072]{1,0:T(8,128)S(1)} %fusion.9), kind=kCustom, calls=%all-reduce-scatter | all-reduce-scatter fusion | flops 393217 | bytes 1376768
  167.9 3.6 %collective-permute-start = (f32[16,3072]{1,0:T(8,128)S(1)}, f32[16,3072]{1,0:T(8,128)S(1)}, u32[]{:S(2)}, u32[]{:S(2)}) collective-permute-start(f32[16,3072]{1,0:T(8,128)S(1)} %fusion), channel_id=1, source_target_pairs={{0,1},{1,2},{2,3},{3,4},{4,5},{5,6},{6,7},{8,9},{9,10},{10,11},{11... | collective-permute-start | bytes 589832
  171.6 3.2 %collective-permute-start.1 = (f32[12,3072]{1,0:T(8,128)S(1)}, f32[12,3072]{1,0:T(8,128)S(1)}, u32[]{:S(2)}, u32[]{:S(2)}) collective-permute-start(f32[12,3072]{1,0:T(8,128)S(1)} %slice), channel_id=1, source_target_pairs={{0,2},{1,3},{2,4},{3,5},{4,6},{5,7},{8,10},{9,11},{10,12},{11,13},... | collective-permute-start | bytes 442376
  174.8 0.0 copy-done.3
  174.8 0.6 dynamic-slice.4
  176.1 2.7 %collective-permute-done.1 = f32[12,3072]{1,0:T(8,128)S(1)} collective-permute-done((f32[12,3072]{1,0:T(8,128)S(1)}, f32[12,3072]{1,0:T(8,128)S(1)}, u32[]{:S(2)}, u32[]{:S(2)}) %collective-permute-start.1) | collective-permute-done | bytes 147488
  178.8 0.0 collective-permute-done
  178.8 0.5 concatenate
  179.3 0.0 copy-done
  179.3 0.0 copy-done.2
  179.3 0.7 fusion.17
  (1 shorter events, 0.0 us)
Async XLA Ops:
  6.5 124.0 %all-reduce.4.cloned.1.call-start = ((), (), s32[]{:S(2)}) async-start(), calls=%async_computation | async-start | bytes 4718592 | tf_op jit(solution)/shard_map/psum | solution.py:10
  35.0 95.5 %copy-start.1 = (f32[6144]{0:T(1024)S(1)}, f32[6144]{0:T(1024)}, u32[]{:S(2)}) copy-start(f32[6144]{0:T(1024)} %param.7) | copy-start | bytes 73732
  35.1 139.8 %copy-start.3 = (u32[32]{0:T(128)S(1)}, u32[32]{0:T(128)}, u32[]{:S(2)}) copy-start(u32[32]{0:T(128)} %constant.11) | copy-start | bytes 388
  146.3 33.0 %copy-start = (bf16[12,3072]{1,0:T(8,128)(2,1)S(1)}, bf16[12,3072]{1,0:T(8,128)(2,1)}, u32[]{:S(2)}) copy-start(bf16[12,3072]{1,0:T(8,128)(2,1)} %param.5) | copy-start | bytes 221188
  146.3 33.0 %copy-start.2 = (f32[3072]{0:T(1024)S(1)}, f32[3072]{0:T(1024)}, u32[]{:S(2)}) copy-start(f32[3072]{0:T(1024)} %param.9) | copy-start | bytes 36868
  167.9 10.9 %collective-permute-start = (f32[16,3072]{1,0:T(8,128)S(1)}, f32[16,3072]{1,0:T(8,128)S(1)}, u32[]{:S(2)}, u32[]{:S(2)}) collective-permute-start(f32[16,3072]{1,0:T(8,128)S(1)} %fusion), channel_id=1, source_target_pairs={{0,1},{1,2},{2,3},{3,4},{4,5},{5,6},{6,7},{8,9},{9,10},{10,11},{11... | collective-permute-start | bytes 589832
  171.6 7.2 %collective-permute-start.1 = (f32[12,3072]{1,0:T(8,128)S(1)}, f32[12,3072]{1,0:T(8,128)S(1)}, u32[]{:S(2)}, u32[]{:S(2)}) collective-permute-start(f32[12,3072]{1,0:T(8,128)S(1)} %slice), channel_id=1, source_target_pairs={{0,2},{1,3},{2,4},{3,5},{4,6},{5,7},{8,10},{9,11},{10,12},{11,13},... | collective-permute-start | bytes 442376
Sparse Core Ops, SparseCore 0:
  35.2 95.3 all-reduce.3
where the time goes:
time: 188 us; the launch traced here: 187 us
  waiting for transfers between devices  98.2 us (52%)
  blocking collectives  33.6 us (18%)
  matrix products  32 us (17%)
  between operations  14.1 us (8%)
  starting transfers between devices  6.88 us (4%)
    psum x1, waiting for transfers between devices, on_device(): summed_up = lax.psum(partial_up, 'row')  95.5 us
    unnamed x1, blocking collectives  21.6 us
    dot_general x1, matrix products, on_device(): jnp.dot(gathered, up_weight, preferred_element_type=jnp.float32)  16.3 us
    dot_general x1, matrix products, on_device(): jnp.dot(activated, down_weight, preferred_element_type=jnp.float32)  15.7 us
    all_gather x1, blocking collectives, on_device(): gathered = lax.all_gather(tokens, 'col', axis=0, tiled=True)  12.1 us
    unnamed x2, starting transfers between devices  6.88 us
  transfers between devices with their start and end apart: 3, of which 2 were waited for; matrix products, arithmetic and copies ran while one was open for 0% of the time, Pallas kernels for 0%

commit v1 on v0

v1 whole, which is shorter than its diff:
```python
import functools

import jax
import jax.numpy as jnp
from jax import lax
from jax.experimental import pallas as pl
from jax.experimental.pallas import tpu as pltpu
from jax.sharding import PartitionSpec as P

CHUNK = 256
SPLIT = 4
MESH = pl.DeviceIdType.MESH


def gelu(v):
    return 0.5 * v * (1.0 + jnp.tanh(0.7978845608028654 * (v + 0.044715 * (v * v * v))))


def kernel(
    rows, cols, tok_ref, up_ref, ub_ref, down_ref, db_ref, out_ref,
    ubuf, dbuf, gath, xg, part, sbuf, rin, rc, act, acc, packf, own, sib_out, sib_in, peer_out, peer_in,
    usem, dsem, g_send, g_recv, f_send, in_send, in_recv, out_send, c_recv,
    s1_send, s1_recv, s2_send, s2_recv,
):
    tok, feat = tok_ref.shape
    wide = feat // SPLIT
    n = up_ref.shape[1] // CHUNK
    u_slots, d_slots = ubuf.shape[0], dbuf.shape[0]
    chips = cols // 2
    half = rows // 2
    r, c = lax.axis_index("row"), lax.axis_index("col")
    chip, core = c // 2, lax.rem(c, 2)
    sib = chip * 2 + 1 - core
    low = r < half
    depth = jnp.where(low, half - 1 - r, r - half)
    inner = jnp.where(low, r + 1, r - 1)
    outer = jnp.where(low, r - 1, r + 1)
    centre, end = depth == 0, depth == half - 1

    def peer(k):
        return lax.rem(chip + k, chips)

    def load_up(j):
        at = pl.ds(pl.multiple_of(j * CHUNK, CHUNK), CHUNK)
        slot = lax.rem(j, u_slots)
        return pltpu.make_async_copy(up_ref.at[:, at], ubuf.at[slot], usem.at[slot])

    def load_down(j):
        at = pl.ds(pl.multiple_of(j * CHUNK, CHUNK), CHUNK)
        slot = lax.rem(j, d_slots)
        return pltpu.make_async_copy(down_ref.at[at, :], dbuf.at[slot], dsem.at[slot])

    def each(lo, hi, body):
        def step(i, carry):
            body(i)
            return carry
        lax.fori_loop(lo, hi, step, 0)

    each(0, u_slots, lambda j: load_up(j).start())

    barrier = pltpu.get_barrier_semaphore()

    def greet(row, col):
        pl.semaphore_signal(barrier, inc=1, device_id=(row, col), device_id_type=MESH)

    greet(r, sib)
    each(1, chips, lambda k: greet(r, peer(k) * 2 + core))
    greet(inner, c)

    @pl.when(jnp.logical_not(end))
    def _():
        greet(outer, c)

    mine = tok_ref[...].astype(jnp.float32)
    own[...] = jnp.zeros_like(own)
    for q in range(SPLIT):
        own[q * tok:(q + 1) * tok, :] = mine[:, q * wide:(q + 1) * wide]
    gath[c] = own[...].astype(jnp.bfloat16)

    @pl.when(end)
    def _():
        pl.semaphore_wait(barrier, chips + 1)

    @pl.when(jnp.logical_not(end))
    def _():
        pl.semaphore_wait(barrier, chips + 2)

    def gather_copy(src, send, col):
        return pltpu.make_async_remote_copy(
            src_ref=gath.at[src], dst_ref=gath.at[src], send_sem=send, recv_sem=g_recv.at[src],
            device_id=(r, col), device_id_type=MESH)

    each(1, chips, lambda k: gather_copy(c, g_send.at[k], peer(k) * 2 + core).start())
    gather_copy(c, g_send.at[0], sib).start()

    def forward(k):
        src = peer(k) * 2 + core
        gather_copy(src, f_send.at[k], sib).wait_recv()
        gather_copy(src, f_send.at[k], sib).start()

    each(1, chips, forward)
    each(0, d_slots, lambda j: load_down(j).start())
    each(0, chips, lambda k: gather_copy(peer(k) * 2 + 1 - core, g_send.at[0], sib).wait_recv())
    each(1, chips, lambda k: gather_copy(c, g_send.at[k], sib).wait_send())
    gather_copy(c, g_send.at[0], sib).wait_send()
    each(1, chips, lambda k: gather_copy(peer(k) * 2 + core, f_send.at[k], sib).wait_send())

    for d in range(cols):
        slab = gath[d].astype(jnp.float32)
        for q in range(SPLIT):
            acc[d * tok:(d + 1) * tok, q * wide:(q + 1) * wide] = slab[q * tok:(q + 1) * tok, :]
    xg[...] = acc[...].astype(jnp.bfloat16)
    acc[...] = jnp.zeros_like(acc)

    def inward(j, dst, sem):
        return pltpu.make_async_remote_copy(
            src_ref=sbuf.at[j], dst_ref=dst.at[j], send_sem=in_send.at[j], recv_sem=sem.at[j],
            device_id=(inner, c), device_id_type=MESH)

    def outward(j):
        return pltpu.make_async_remote_copy(
            src_ref=act.at[j], dst_ref=rc.at[j], send_sem=out_send.at[j], recv_sem=c_recv.at[j],
            device_id=(outer, c), device_id_type=MESH)

    lag_in = 2 * (half - 1 - depth)
    lag_out = 2 * (half - 1) + 3 + 3 * depth
    ticks = n + 2 * (half - 1) + 3 + 3 * (half - 1)

    def tick(t):
        @pl.when(t < n)
        def _():
            load_up(t).wait()
            part[t] = jnp.dot(xg[...], ubuf[lax.rem(t, u_slots)], preferred_element_type=jnp.float32)

            @pl.when(t + u_slots < n)
            def _():
                load_up(t + u_slots).start()

        a = t - lag_in

        @pl.when((a >= 0) & (a < n))
        def _():
            @pl.when(jnp.logical_not(end))
            def _():
                inward(a, rin, in_recv).wait_recv()
                part[a] = part[a] + rin[a].astype(jnp.float32)

            sbuf[a] = part[a].astype(jnp.bfloat16)

            @pl.when(centre)
            def _():
                inward(a, rc, c_recv).start()

            @pl.when(jnp.logical_not(centre))
            def _():
                inward(a, rin, in_recv).start()

        b = t - lag_out

        @pl.when((b >= 0) & (b < n))
        def _():
            outward(b).wait_recv()

            @pl.when(centre)
            def _():
                bias = ub_ref[:, pl.ds(pl.multiple_of(b * CHUNK, CHUNK), CHUNK)]
                act[b] = gelu(part[b] + rc[b].astype(jnp.float32) + bias).astype(jnp.bfloat16)

            @pl.when(jnp.logical_not(centre))
            def _():
                act[b] = rc[b]

            @pl.when(jnp.logical_not(end))
            def _():
                outward(b).start()

            load_down(b).wait()
            acc[...] += jnp.dot(act[b], dbuf[lax.rem(b, d_slots)], preferred_element_type=jnp.float32)

            @pl.when(b + d_slots < n)
            def _():
                load_down(b + d_slots).start()

    each(0, ticks, tick)

    packf[...] = jnp.zeros_like(packf)
    for d in range(cols):
        for q in range(SPLIT):
            packf[d, q * tok:(q + 1) * tok, :] = acc[d * tok:(d + 1) * tok, q * wide:(q + 1) * wide]

    def to_sibling(k):
        return pltpu.make_async_remote_copy(
            src_ref=sib_out.at[k], dst_ref=sib_in.at[k], send_sem=s1_send.at[k], recv_sem=s1_recv.at[k],
            device_id=(r, sib), device_id_type=MESH)

    def to_peer(k):
        return pltpu.make_async_remote_copy(
            src_ref=peer_out.at[k], dst_ref=peer_in.at[k], send_sem=s2_send.at[k], recv_sem=s2_recv.at[k],
            device_id=(r, peer(k) * 2 + core), device_id_type=MESH)

    def first(i):
        k = lax.rem(i, chips)
        sib_out[k] = packf[peer(k) * 2 + 1 - core].astype(jnp.bfloat16)
        to_sibling(k).start()

    def second(k):
        to_sibling(k).wait_recv()
        peer_out[k] = (packf[peer(k) * 2 + core] + sib_in[k].astype(jnp.float32)).astype(jnp.bfloat16)
        to_peer(k).start()

    each(1, chips + 1, first)
    each(1, chips, second)
    to_sibling(0).wait_recv()
    own[...] = packf[c] + sib_in[0].astype(jnp.float32)

    def third(k):
        to_peer(k).wait_recv()
        own[...] += peer_in[k].astype(jnp.float32)

    each(1, chips, third)
    for q in range(SPLIT):
        at = slice(q * wide, (q + 1) * wide)
        out_ref[:, at] = (
            tok_ref[:, at].astype(jnp.float32) + own[q * tok:(q + 1) * tok, :] + db_ref[:, at]
        ).astype(out_ref.dtype)

    each(0, chips, lambda k: to_sibling(k).wait_send())
    each(1, chips, lambda k: to_peer(k).wait_send())
    each(0, n, lambda j: inward(j, rin, in_recv).wait_send())

    @pl.when(jnp.logical_not(end))
    def _():
        each(0, n, lambda j: outward(j).wait_send())


def on_device(rows, cols, tokens, up_weight, up_bias, down_weight, down_bias):
    tok, feat = tokens.shape
    hidden = up_weight.shape[1]
    n = hidden // CHUNK
    m = tok * cols
    chips = cols // 2
    chunk_bytes = feat * CHUNK * 2
    u_slots = max(1, min(n, 28 * 1024 * 1024 // chunk_bytes))
    d_slots = max(1, min(n, 18 * 1024 * 1024 // chunk_bytes))
    tall = -(-tok * SPLIT // 16) * 16
    wide = feat // SPLIT
    bf16, f32 = jnp.bfloat16, jnp.float32
    vmem, dma = pltpu.VMEM, pltpu.SemaphoreType.DMA
    in_vmem = pl.BlockSpec(memory_space=pltpu.VMEM)
    in_place = pl.BlockSpec(memory_space=pl.ANY)
    return pl.pallas_call(
        functools.partial(kernel, rows, cols),
        out_shape=jax.ShapeDtypeStruct((tok, feat), bf16),
        in_specs=[in_vmem, in_place, in_vmem, in_place, in_vmem],
        out_specs=in_vmem,
        scratch_shapes=[
            vmem((u_slots, feat, CHUNK), bf16),
            vmem((d_slots, CHUNK, feat), bf16),
            vmem((cols, tall, wide), bf16),
            vmem((m, feat), bf16),
            vmem((n, m, CHUNK), f32),
            vmem((n, m, CHUNK), bf16),
            vmem((n, m, CHUNK), bf16),
            vmem((n, m, CHUNK), bf16),
            vmem((n, m, CHUNK), bf16),
            vmem((m, feat), f32),
            vmem((cols, tall, wide), f32),
            vmem((tall, wide), f32),
            vmem((chips, tall, wide), bf16),
            vmem((chips, tall, wide), bf16),
            vmem((chips, tall, wide), bf16),
            vmem((chips, tall, wide), bf16),
            dma((u_slots,)),
            dma((d_slots,)),
            dma((chips,)),
            dma((cols,)),
            dma((chips,)),
            dma((n,)),
            dma((n,)),
            dma((n,)),
            dma((n,)),
            dma((chips,)),
            dma((chips,)),
            dma((chips,)),
            dma((chips,)),
        ],
        cost_estimate=pl.CostEstimate(
            flops=4 * m * feat * hidden, bytes_accessed=4 * feat * hidden, transcendentals=m * hidden),
        compiler_params=pltpu.CompilerParams(
            collective_id=0, has_side_effects=True, vmem_limit_bytes=63 * 1024 * 1024),
    )(tokens, up_weight, up_bias.reshape(1, -1), down_weight, down_bias.reshape(1, -1))


def solution(mesh):
    placed = (P("col", "row"), P("row", "col"), P("col"), P("col", "row"), P("row"))
    body = functools.partial(on_device, mesh.shape["row"], mesh.shape["col"])
    return jax.shard_map(body, mesh=mesh, in_specs=placed, out_specs=P("col", "row"), check_vma=False)
```

time: 188 us -> 60.4 us (0.32)
  waiting for transfers between devices: 98.2 us -> 0 us
  Pallas kernels: 0 us -> 58.5 us
  blocking collectives: 33.6 us -> 0 us
  matrix products: 32 us -> 0 us
  between operations: 14.1 us -> 0.01 us
  starting transfers between devices: 6.88 us -> 0 us
    psum x1 -> x0, waiting for transfers between devices: 95.5 us -> none  [on_device(): summed_up = lax.psum(partial_up, 'row')]
    pallas_call x0 -> x1, Pallas kernels: none -> 58.5 us  [on_device(): pl.pallas_call(functools.partial(kernel, rows, cols), out_shape=jax.Shape...]
    dot_general x2 -> x0, matrix products: 32 us -> none  [the longest x1 16.3 us: on_device(): jnp.dot(gathered, up_weight, preferred_element_type=jnp.float32)]
    unnamed x1 -> x0, blocking collectives: 21.6 us -> none
    all_gather x1 -> x0, blocking collectives: 12.1 us -> none  [on_device(): gathered = lax.all_gather(tokens, 'col', axis=0, tiled=True)]
    unnamed x2 -> x0, starting transfers between devices: 6.88 us -> none
    unnamed x3 -> x0, waiting for transfers between devices: 2.72 us -> none
  transfers between devices with their start and end apart: 3 -> 0, of which waited for: 2 -> 0; matrix products, arithmetic and copies ran while one was open for 0% -> 0% of each run, Pallas kernels for 0% -> 0%
where the time goes in v1:
time: 60.4 us; the launch traced here: 60 us
  Pallas kernels  58.5 us (97%)
  local copies, waits for them, and re-layouts  1.54 us (3%)
    pallas_call x1, Pallas kernels, on_device(): pl.pallas_call(functools.partial(kernel, rows, cols), out_shape=jax.Shape...  58.5 us
    unnamed x1, local copies, waits for them, and re-layouts  1.54 us

profile of v1, /device:TPU:1, one launch (start us, length us, event | category | flops | bytes accessed | tf_op | source)
XLA Modules:
  0.0 60.0 jit_solution(1299693229256891065)
XLA Ops:
  0.0 58.5 %shard_map.55 = bf16[12,3072]{1,0:T(8,128)(2,1)} custom-call(bf16[12,3072]{1,0:T(8,128)(2,1)} %tok_ref.1, bf16[3072,6144]{1,0:T(8,128)(2,1)} %up_ref.1, f32[1,6144]{1,0:T(1,128)} %bitcast.2, bf16[6144,3072]{1,0:T(8,128)(2,1)} %down_ref.1, f32[1,3072]{1,0:T(1,128)} %bitcast.3), custom_call_target="tpu_custom_call" | custom-call | flops 7247757312 | bytes 75497472 | tf_op jit(solution)/shard_map/pallas_call | solution.py:251
  58.5 1.5 %copy.7 = bf16[12,3072]{1,0:T(8,128)(2,1)} copy(bf16[12,3072]{1,0:T(8,128)(2,1)} %shard_map.55) | data formatting | bytes 147456

commit v2 on v1

--- a/solution.py
+++ b/solution.py
@@ -56,8 +56,6 @@
             return carry
         lax.fori_loop(lo, hi, step, 0)
 
-    each(0, u_slots, lambda j: load_up(j).start())
-
     barrier = pltpu.get_barrier_semaphore()
 
     def greet(row, col):
@@ -70,6 +68,9 @@
     @pl.when(jnp.logical_not(end))
     def _():
         greet(outer, c)
+
+    early = min(6, u_slots)
+    each(0, early, lambda j: load_up(j).start())
 
     mine = tok_ref[...].astype(jnp.float32)
     own[...] = jnp.zeros_like(own)
@@ -92,6 +93,7 @@
 
     each(1, chips, lambda k: gather_copy(c, g_send.at[k], peer(k) * 2 + core).start())
     gather_copy(c, g_send.at[0], sib).start()
+    each(early, u_slots, lambda j: load_up(j).start())
 
     def forward(k):
         src = peer(k) * 2 + core
@@ -122,11 +124,49 @@
             src_ref=act.at[j], dst_ref=rc.at[j], send_sem=out_send.at[j], recv_sem=c_recv.at[j],
             device_id=(outer, c), device_id_type=MESH)
 
-    lag_in = 2 * (half - 1 - depth)
-    lag_out = 2 * (half - 1) + 3 + 3 * depth
-    ticks = n + 2 * (half - 1) + 3 + 3 * (half - 1)
+    lag_in = 1 + 4 * (half - 1 - depth)
+    lag_out = 4 * half + 6 * depth
+    ticks = n + 4 * half + 6 * (half - 1)
 
     def tick(t):
+        a = t - lag_in
+
+        @pl.when((a >= 0) & (a < n))
+        def _():
+            @pl.when(jnp.logical_not(end))
+            def _():
+                inward(a, rin, in_recv).wait_recv()
+                part[a] = part[a] + rin[a].astype(jnp.float32)
+
+            sbuf[a] = part[a].astype(jnp.bfloat16)
+
+            @pl.when(centre)
+            def _():
+                inward(a, rc, c_recv).start()
+
+            @pl.when(jnp.logical_not(centre))
+            def _():
+                inward(a, rin, in_recv).start()
+
+        b = t - lag_out
+
+        @pl.when((b >= 0) & (b < n))
+        def _():
+            outward(b).wait_recv()
+
+            @pl.when(centre)
+            def _():
+                bias = ub_ref[:, pl.ds(pl.multiple_of(b * CHUNK, CHUNK), CHUNK)]
+                act[b] = gelu(part[b] + rc[b].astype(jnp.float32) + bias).astype(jnp.bfloat16)
+
+            @pl.when(jnp.logical_not(centre))
+            def _():
+                act[b] = rc[b]
+
+            @pl.when(jnp.logical_not(end))
+            def _():
+                outward(b).start()
+
         @pl.when(t < n)
         def _():
             load_up(t).wait()
@@ -136,44 +176,8 @@
             def _():
                 load_up(t + u_slots).start()
 
-        a = t - lag_in
-
-        @pl.when((a >= 0) & (a < n))
-        def _():
-            @pl.when(jnp.logical_not(end))
-            def _():
-                inward(a, rin, in_recv).wait_recv()
-                part[a] = part[a] + rin[a].astype(jnp.float32)
-
-            sbuf[a] = part[a].astype(jnp.bfloat16)
-
-            @pl.when(centre)
-            def _():
-                inward(a, rc, c_recv).start()
-
-            @pl.when(jnp.logical_not(centre))
-            def _():
-                inward(a, rin, in_recv).start()
-
-        b = t - lag_out
-
         @pl.when((b >= 0) & (b < n))
         def _():
-            outward(b).wait_recv()
-
-            @pl.when(centre)
-            def _():
-                bias = ub_ref[:, pl.ds(pl.multiple_of(b * CHUNK, CHUNK), CHUNK)]
-                act[b] = gelu(part[b] + rc[b].astype(jnp.float32) + bias).astype(jnp.bfloat16)
-
-            @pl.when(jnp.logical_not(centre))
-            def _():
-                act[b] = rc[b]
-
-            @pl.when(jnp.logical_not(end))
-            def _():
-                outward(b).start()
-
             load_down(b).wait()
             acc[...] += jnp.dot(act[b], dbuf[lax.rem(b, d_slots)], preferred_element_type=jnp.float32)
 
@@ -183,7 +187,8 @@
 
     each(0, ticks, tick)
 
-    packf[...] = jnp.zeros_like(packf)
+    if packf.shape[1] != SPLIT * tok:
+        packf[...] = jnp.zeros_like(packf)
     for d in range(cols):
         for q in range(SPLIT):
             packf[d, q * tok:(q + 1) * tok, :] = acc[d * tok:(d + 1) * tok, q * wide:(q + 1) * wide]

time: 60.4 us -> 56.9 us (0.942)
  Pallas kernels: 58.5 us -> 55 us
    pallas_call x1, Pallas kernels: 58.5 us -> 55 us  [on_device(): pl.pallas_call(functools.partial(kernel, rows, cols), out_shape=jax.Shape...]
where the time goes in v2:
time: 56.9 us; the launch traced here: 56.6 us
  Pallas kernels  55 us (97%)
  local copies, waits for them, and re-layouts  1.54 us (3%)
    pallas_call x1, Pallas kernels, on_device(): pl.pallas_call(functools.partial(kernel, rows, cols), out_shape=jax.Shape...  55 us
    unnamed x1, local copies, waits for them, and re-layouts  1.54 us

profile of v2, /device:TPU:1, one launch (start us, length us, event | category | flops | bytes accessed | tf_op | source)
XLA Modules:
  0.0 56.6 jit_solution(5756362850076418873)
XLA Ops:
  0.0 55.0 %shard_map.55 = bf16[12,3072]{1,0:T(8,128)(2,1)} custom-call(bf16[12,3072]{1,0:T(8,128)(2,1)} %tok_ref.1, bf16[3072,6144]{1,0:T(8,128)(2,1)} %up_ref.1, f32[1,6144]{1,0:T(1,128)} %bitcast.2, bf16[6144,3072]{1,0:T(8,128)(2,1)} %down_ref.1, f32[1,3072]{1,0:T(1,128)} %bitcast.3), custom_call_target="tpu_custom_call" | custom-call | flops 7247757312 | bytes 75497472 | tf_op jit(solution)/shard_map/pallas_call | solution.py:256
  55.0 1.5 %copy.7 = bf16[12,3072]{1,0:T(8,128)(2,1)} copy(bf16[12,3072]{1,0:T(8,128)(2,1)} %shard_map.55) | data formatting | bytes 147456

commit v3 on v2

--- a/solution.py
+++ b/solution.py
@@ -18,7 +18,7 @@
 
 def kernel(
     rows, cols, tok_ref, up_ref, ub_ref, down_ref, db_ref, out_ref,
-    ubuf, dbuf, gath, xg, part, sbuf, rin, rc, act, acc, packf, own, sib_out, sib_in, peer_out, peer_in,
+    ubuf, dbuf, gath, xg, part, sbuf, rin, rc, act, acc, own, packf, sib_out, sib_in, peer_out, peer_in,
     usem, dsem, g_send, g_recv, f_send, in_send, in_recv, out_send, c_recv,
     s1_send, s1_recv, s2_send, s2_recv,
 ):
@@ -27,6 +27,9 @@
     n = up_ref.shape[1] // CHUNK
     u_slots, d_slots = ubuf.shape[0], dbuf.shape[0]
     chips = cols // 2
+    near = chips * tok
+    halves, _, span = sib_out.shape
+    narrow = span // SPLIT
     half = rows // 2
     r, c = lax.axis_index("row"), lax.axis_index("col")
     chip, core = c // 2, lax.rem(c, 2)
@@ -74,9 +77,10 @@
 
     mine = tok_ref[...].astype(jnp.float32)
     own[...] = jnp.zeros_like(own)
+    packf[...] = jnp.zeros_like(packf)
     for q in range(SPLIT):
         own[q * tok:(q + 1) * tok, :] = mine[:, q * wide:(q + 1) * wide]
-    gath[c] = own[...].astype(jnp.bfloat16)
+    gath[0] = own[...].astype(jnp.bfloat16)
 
     @pl.when(end)
     def _():
@@ -86,33 +90,29 @@
     def _():
         pl.semaphore_wait(barrier, chips + 2)
 
-    def gather_copy(src, send, col):
-        return pltpu.make_async_remote_copy(
-            src_ref=gath.at[src], dst_ref=gath.at[src], send_sem=send, recv_sem=g_recv.at[src],
-            device_id=(r, col), device_id_type=MESH)
-
-    each(1, chips, lambda k: gather_copy(c, g_send.at[k], peer(k) * 2 + core).start())
-    gather_copy(c, g_send.at[0], sib).start()
+    def gather_copy(k):
+        return pltpu.make_async_remote_copy(
+            src_ref=gath.at[0], dst_ref=gath.at[chips - k], send_sem=g_send.at[k], recv_sem=g_recv.at[chips - k],
+            device_id=(r, peer(k) * 2 + core), device_id_type=MESH)
+
+    swap = pltpu.make_async_remote_copy(
+        src_ref=xg.at[pl.ds(0, near)], dst_ref=xg.at[pl.ds(near, near)], send_sem=f_send.at[0], recv_sem=f_send.at[1],
+        device_id=(r, sib), device_id_type=MESH)
+
+    each(1, chips, lambda k: gather_copy(k).start())
     each(early, u_slots, lambda j: load_up(j).start())
-
-    def forward(k):
-        src = peer(k) * 2 + core
-        gather_copy(src, f_send.at[k], sib).wait_recv()
-        gather_copy(src, f_send.at[k], sib).start()
-
-    each(1, chips, forward)
+    for k in range(chips):
+        if k > 0:
+            gather_copy(chips - k).wait_recv()
+        slab = gath[k].astype(jnp.float32)
+        for q in range(SPLIT):
+            acc[k * tok:(k + 1) * tok, q * wide:(q + 1) * wide] = slab[q * tok:(q + 1) * tok, :]
+    xg[0:near] = acc[0:near].astype(jnp.bfloat16)
+    swap.start()
     each(0, d_slots, lambda j: load_down(j).start())
-    each(0, chips, lambda k: gather_copy(peer(k) * 2 + 1 - core, g_send.at[0], sib).wait_recv())
-    each(1, chips, lambda k: gather_copy(c, g_send.at[k], sib).wait_send())
-    gather_copy(c, g_send.at[0], sib).wait_send()
-    each(1, chips, lambda k: gather_copy(peer(k) * 2 + core, f_send.at[k], sib).wait_send())
-
-    for d in range(cols):
-        slab = gath[d].astype(jnp.float32)
-        for q in range(SPLIT):
-            acc[d * tok:(d + 1) * tok, q * wide:(q + 1) * wide] = slab[q * tok:(q + 1) * tok, :]
-    xg[...] = acc[...].astype(jnp.bfloat16)
     acc[...] = jnp.zeros_like(acc)
+    each(1, chips, lambda k: gather_copy(k).wait_send())
+    swap.wait()
 
     def inward(j, dst, sem):
         return pltpu.make_async_remote_copy(
@@ -187,50 +187,45 @@
 
     each(0, ticks, tick)
 
-    if packf.shape[1] != SPLIT * tok:
-        packf[...] = jnp.zeros_like(packf)
-    for d in range(cols):
-        for q in range(SPLIT):
-            packf[d, q * tok:(q + 1) * tok, :] = acc[d * tok:(d + 1) * tok, q * wide:(q + 1) * wide]
-
-    def to_sibling(k):
-        return pltpu.make_async_remote_copy(
-            src_ref=sib_out.at[k], dst_ref=sib_in.at[k], send_sem=s1_send.at[k], recv_sem=s1_recv.at[k],
+    def to_sibling(h):
+        return pltpu.make_async_remote_copy(
+            src_ref=sib_out.at[h], dst_ref=sib_in.at[h], send_sem=s1_send.at[h], recv_sem=s1_recv.at[h],
             device_id=(r, sib), device_id_type=MESH)
 
-    def to_peer(k):
-        return pltpu.make_async_remote_copy(
-            src_ref=peer_out.at[k], dst_ref=peer_in.at[k], send_sem=s2_send.at[k], recv_sem=s2_recv.at[k],
+    def to_peer(h, k):
+        there = h * chips + chips - k
+        return pltpu.make_async_remote_copy(
+            src_ref=peer_out.at[h * chips + k], dst_ref=peer_in.at[there],
+            send_sem=s2_send.at[h * chips + k], recv_sem=s2_recv.at[there],
             device_id=(r, peer(k) * 2 + core), device_id_type=MESH)
 
-    def first(i):
-        k = lax.rem(i, chips)
-        sib_out[k] = packf[peer(k) * 2 + 1 - core].astype(jnp.bfloat16)
-        to_sibling(k).start()
-
-    def second(k):
-        to_sibling(k).wait_recv()
-        peer_out[k] = (packf[peer(k) * 2 + core] + sib_in[k].astype(jnp.float32)).astype(jnp.bfloat16)
-        to_peer(k).start()
-
-    each(1, chips + 1, first)
-    each(1, chips, second)
-    to_sibling(0).wait_recv()
-    own[...] = packf[c] + sib_in[0].astype(jnp.float32)
-
-    def third(k):
-        to_peer(k).wait_recv()
-        own[...] += peer_in[k].astype(jnp.float32)
-
-    each(1, chips, third)
-    for q in range(SPLIT):
-        at = slice(q * wide, (q + 1) * wide)
-        out_ref[:, at] = (
-            tok_ref[:, at].astype(jnp.float32) + own[q * tok:(q + 1) * tok, :] + db_ref[:, at]
-        ).astype(out_ref.dtype)
-
-    each(0, chips, lambda k: to_sibling(k).wait_send())
-    each(1, chips, lambda k: to_peer(k).wait_send())
+    for h in range(halves):
+        sib_out[h] = acc[near:2 * near, h * span:(h + 1) * span].astype(jnp.bfloat16)
+        to_sibling(h).start()
+    for h in range(halves):
+        at = slice(h * span, (h + 1) * span)
+        to_sibling(h).wait_recv()
+        acc[0:near, at] = acc[0:near, at] + sib_in[h].astype(jnp.float32)
+        for k in range(1, chips):
+            for q in range(SPLIT):
+                lo = h * span + q * narrow
+                packf[q * tok:(q + 1) * tok, :] = acc[k * tok:(k + 1) * tok, lo:lo + narrow]
+            peer_out[h * chips + k] = packf[...].astype(jnp.bfloat16)
+            to_peer(h, k).start()
+    for h in range(halves):
+        at = slice(h * span, (h + 1) * span)
+        acc[0:tok, at] = acc[0:tok, at] + (tok_ref[:, at].astype(jnp.float32) + db_ref[:, at])
+        for k in range(1, chips):
+            to_peer(h, chips - k).wait_recv()
+            slab = peer_in[h * chips + k].astype(jnp.float32)
+            for q in range(SPLIT):
+                lo = h * span + q * narrow
+                acc[0:tok, lo:lo + narrow] = acc[0:tok, lo:lo + narrow] + slab[q * tok:(q + 1) * tok, :]
+        out_ref[:, at] = acc[0:tok, at].astype(out_ref.dtype)
+
+    for h in range(halves):
+        to_sibling(h).wait_send()
+        each(1, chips, lambda k, h=h: to_peer(h, k).wait_send())
     each(0, n, lambda j: inward(j, rin, in_recv).wait_send())
 
     @pl.when(jnp.logical_not(end))
@@ -249,6 +244,8 @@
     d_slots = max(1, min(n, 18 * 1024 * 1024 // chunk_bytes))
     tall = -(-tok * SPLIT // 16) * 16
     wide = feat // SPLIT
+    halves = 2 if feat % (2 * SPLIT * 128) == 0 else 1
+    span = feat // halves
     bf16, f32 = jnp.bfloat16, jnp.float32
     vmem, dma = pltpu.VMEM, pltpu.SemaphoreType.DMA
     in_vmem = pl.BlockSpec(memory_space=pltpu.VMEM)
@@ -261,7 +258,7 @@
         scratch_shapes=[
             vmem((u_slots, feat, CHUNK), bf16),
             vmem((d_slots, CHUNK, feat), bf16),
-            vmem((cols, tall, wide), bf16),
+            vmem((chips, tall, wide), bf16),
             vmem((m, feat), bf16),
             vmem((n, m, CHUNK), f32),
             vmem((n, m, CHUNK), bf16),
@@ -269,25 +266,25 @@
             vmem((n, m, CHUNK), bf16),
             vmem((n, m, CHUNK), bf16),
             vmem((m, feat), f32),
-            vmem((cols, tall, wide), f32),
             vmem((tall, wide), f32),
-            vmem((chips, tall, wide), bf16),
-            vmem((chips, tall, wide), bf16),
-            vmem((chips, tall, wide), bf16),
-            vmem((chips, tall, wide), bf16),
+            vmem((tall, span // SPLIT), f32),
+            vmem((halves, m // 2, span), bf16),
+            vmem((halves, m // 2, span), bf16),
+            vmem((halves * chips, tall, span // SPLIT), bf16),
+            vmem((halves * chips, tall, span // SPLIT), bf16),
             dma((u_slots,)),
             dma((d_slots,)),
             dma((chips,)),
-            dma((cols,)),
             dma((chips,)),
-            dma((n,)),
-            dma((n,)),
-            dma((n,)),
-            dma((n,)),
-            dma((chips,)),
-            dma((chips,)),
-            dma((chips,)),
-            dma((chips,)),
+            dma((2,)),
+            dma((n,)),
+            dma((n,)),
+            dma((n,)),
+            dma((n,)),
+            dma((halves,)),
+            dma((halves,)),
+            dma((halves * chips,)),
+            dma((halves * chips,)),
         ],
         cost_estimate=pl.CostEstimate(
             flops=4 * m * feat * hidden, bytes_accessed=4 * feat * hidden, transcendentals=m * hidden),

time: 56.9 us -> 56.8 us (level)
  no operation moved by 1% of the time
where the time goes in v3:
time: 56.8 us; the launch traced here: 56.7 us
  Pallas kernels  55.1 us (97%)
  local copies, waits for them, and re-layouts  1.54 us (3%)
    pallas_call x1, Pallas kernels, on_device(): pl.pallas_call(functools.partial(kernel, rows, cols), out_shape=jax.Shape...  55.1 us
    unnamed x1, local copies, waits for them, and re-layouts  1.54 us

profile of v3, /device:TPU:1, one launch (start us, length us, event | category | flops | bytes accessed | tf_op | source)
XLA Modules:
  0.0 56.7 jit_solution(4740919844390951722)
XLA Ops:
  0.0 55.1 %shard_map.55 = bf16[12,3072]{1,0:T(8,128)(2,1)} custom-call(bf16[12,3072]{1,0:T(8,128)(2,1)} %tok_ref.1, bf16[3072,6144]{1,0:T(8,128)(2,1)} %up_ref.1, f32[1,6144]{1,0:T(1,128)} %bitcast.2, bf16[6144,3072]{1,0:T(8,128)(2,1)} %down_ref.1, f32[1,3072]{1,0:T(1,128)} %bitcast.3), custom_call_target="tpu_custom_call" | custom-call | flops 7247757312 | bytes 75497472 | tf_op jit(solution)/shard_map/pallas_call | solution.py:253
  55.1 1.5 %copy.7 = bf16[12,3072]{1,0:T(8,128)(2,1)} copy(bf16[12,3072]{1,0:T(8,128)(2,1)} %shard_map.55) | data formatting | bytes 147456

commit v4 on v3

--- a/solution.py
+++ b/solution.py
@@ -7,7 +7,7 @@
 from jax.experimental.pallas import tpu as pltpu
 from jax.sharding import PartitionSpec as P
 
-CHUNK = 256
+PIECE = 256
 SPLIT = 4
 MESH = pl.DeviceIdType.MESH
 
@@ -24,7 +24,9 @@
 ):
     tok, feat = tok_ref.shape
     wide = feat // SPLIT
-    n = up_ref.shape[1] // CHUNK
+    chunk = ubuf.shape[2]
+    n = up_ref.shape[1] // chunk
+    pieces = chunk // PIECE
     u_slots, d_slots = ubuf.shape[0], dbuf.shape[0]
     chips = cols // 2
     near = chips * tok
@@ -44,12 +46,12 @@
         return lax.rem(chip + k, chips)
 
     def load_up(j):
-        at = pl.ds(pl.multiple_of(j * CHUNK, CHUNK), CHUNK)
+        at = pl.ds(pl.multiple_of(j * chunk, chunk), chunk)
         slot = lax.rem(j, u_slots)
         return pltpu.make_async_copy(up_ref.at[:, at], ubuf.at[slot], usem.at[slot])
 
     def load_down(j):
-        at = pl.ds(pl.multiple_of(j * CHUNK, CHUNK), CHUNK)
+        at = pl.ds(pl.multiple_of(j * chunk, chunk), chunk)
         slot = lax.rem(j, d_slots)
         return pltpu.make_async_copy(down_ref.at[at, :], dbuf.at[slot], dsem.at[slot])
 
@@ -72,7 +74,7 @@
     def _():
         greet(outer, c)
 
-    early = min(6, u_slots)
+    early = min(3, u_slots)
     each(0, early, lambda j: load_up(j).start())
 
     mine = tok_ref[...].astype(jnp.float32)
@@ -119,53 +121,63 @@
             src_ref=sbuf.at[j], dst_ref=dst.at[j], send_sem=in_send.at[j], recv_sem=sem.at[j],
             device_id=(inner, c), device_id_type=MESH)
 
-    def outward(j):
-        return pltpu.make_async_remote_copy(
-            src_ref=act.at[j], dst_ref=rc.at[j], send_sem=out_send.at[j], recv_sem=c_recv.at[j],
+    def outward(j, p):
+        i = j * pieces + p
+        return pltpu.make_async_remote_copy(
+            src_ref=act.at[j, :, pl.ds(p * PIECE, PIECE)], dst_ref=rc.at[i],
+            send_sem=out_send.at[i], recv_sem=c_recv.at[i],
             device_id=(outer, c), device_id_type=MESH)
 
-    lag_in = 1 + 4 * (half - 1 - depth)
-    lag_out = 4 * half + 6 * depth
-    ticks = n + 4 * half + 6 * (half - 1)
+    lag_in = 1 + 2 * (half - 1 - depth)
+    lag_out = 2 * half + 1 + 3 * depth
+    ticks = n + 2 * half + 1 + 3 * (half - 1)
 
     def tick(t):
         a = t - lag_in
 
         @pl.when((a >= 0) & (a < n))
         def _():
-            @pl.when(jnp.logical_not(end))
-            def _():
-                inward(a, rin, in_recv).wait_recv()
-                part[a] = part[a] + rin[a].astype(jnp.float32)
-
-            sbuf[a] = part[a].astype(jnp.bfloat16)
-
-            @pl.when(centre)
-            def _():
-                inward(a, rc, c_recv).start()
-
-            @pl.when(jnp.logical_not(centre))
-            def _():
-                inward(a, rin, in_recv).start()
+            for p in range(pieces):
+                i = a * pieces + p
+                at = slice(p * PIECE, (p + 1) * PIECE)
+
+                @pl.when(jnp.logical_not(end))
+                def _():
+                    inward(i, rin, in_recv).wait_recv()
+                    part[a, :, at] = part[a, :, at] + rin[i].astype(jnp.float32)
+
+                sbuf[i] = part[a, :, at].astype(jnp.bfloat16)
+
+                @pl.when(centre)
+                def _():
+                    inward(i, rc, c_recv).start()
+
+                @pl.when(jnp.logical_not(centre))
+                def _():
+                    inward(i, rin, in_recv).start()
 
         b = t - lag_out
 
         @pl.when((b >= 0) & (b < n))
         def _():
-            outward(b).wait_recv()
-
-            @pl.when(centre)
-            def _():
-                bias = ub_ref[:, pl.ds(pl.multiple_of(b * CHUNK, CHUNK), CHUNK)]
-                act[b] = gelu(part[b] + rc[b].astype(jnp.float32) + bias).astype(jnp.bfloat16)
-
-            @pl.when(jnp.logical_not(centre))
-            def _():
-                act[b] = rc[b]
-
-            @pl.when(jnp.logical_not(end))
-            def _():
-                outward(b).start()
+            for p in range(pieces):
+                i = b * pieces + p
+                at = slice(p * PIECE, (p + 1) * PIECE)
+                outward(b, p).wait_recv()
+
+                @pl.when(centre)
+                def _():
+                    bias = ub_ref[:, pl.ds(pl.multiple_of(i * PIECE, PIECE), PIECE)]
+                    total = part[b, :, at] + rc[i].astype(jnp.float32)
+                    act[b, :, at] = gelu(total + bias).astype(jnp.bfloat16)
+
+                @pl.when(jnp.logical_not(centre))
+                def _():
+                    act[b, :, at] = rc[i]
+
+                @pl.when(jnp.logical_not(end))
+                def _():
+                    outward(b, p).start()
 
         @pl.when(t < n)
         def _():
@@ -226,20 +238,22 @@
     for h in range(halves):
         to_sibling(h).wait_send()
         each(1, chips, lambda k, h=h: to_peer(h, k).wait_send())
-    each(0, n, lambda j: inward(j, rin, in_recv).wait_send())
+    each(0, n * pieces, lambda j: inward(j, rin, in_recv).wait_send())
 
     @pl.when(jnp.logical_not(end))
     def _():
-        each(0, n, lambda j: outward(j).wait_send())
+        for p in range(pieces):
+            each(0, n, lambda j, p=p: outward(j, p).wait_send())
 
 
 def on_device(rows, cols, tokens, up_weight, up_bias, down_weight, down_bias):
     tok, feat = tokens.shape
     hidden = up_weight.shape[1]
-    n = hidden // CHUNK
+    chunk = 2 * PIECE if hidden % (2 * PIECE) == 0 else PIECE
+    n, sent = hidden // chunk, hidden // PIECE
     m = tok * cols
     chips = cols // 2
-    chunk_bytes = feat * CHUNK * 2
+    chunk_bytes = feat * chunk * 2
     u_slots = max(1, min(n, 28 * 1024 * 1024 // chunk_bytes))
     d_slots = max(1, min(n, 18 * 1024 * 1024 // chunk_bytes))
     tall = -(-tok * SPLIT // 16) * 16
@@ -256,15 +270,15 @@
         in_specs=[in_vmem, in_place, in_vmem, in_place, in_vmem],
         out_specs=in_vmem,
         scratch_shapes=[
-            vmem((u_slots, feat, CHUNK), bf16),
-            vmem((d_slots, CHUNK, feat), bf16),
+            vmem((u_slots, feat, chunk), bf16),
+            vmem((d_slots, chunk, feat), bf16),
             vmem((chips, tall, wide), bf16),
             vmem((m, feat), bf16),
-            vmem((n, m, CHUNK), f32),
-            vmem((n, m, CHUNK), bf16),
-            vmem((n, m, CHUNK), bf16),
-            vmem((n, m, CHUNK), bf16),
-            vmem((n, m, CHUNK), bf16),
+            vmem((n, m, chunk), f32),
+            vmem((sent, m, PIECE), bf16),
+            vmem((sent, m, PIECE), bf16),
+            vmem((sent, m, PIECE), bf16),
+            vmem((n, m, chunk), bf16),
             vmem((m, feat), f32),
             vmem((tall, wide), f32),
             vmem((tall, span // SPLIT), f32),
@@ -277,10 +291,10 @@
             dma((chips,)),
             dma((chips,)),
             dma((2,)),
-            dma((n,)),
-            dma((n,)),
-            dma((n,)),
-            dma((n,)),
+            dma((sent,)),
+            dma((sent,)),
+            dma((sent,)),
+            dma((sent,)),
             dma((halves,)),
             dma((halves,)),
             dma((halves * chips,)),

time: 56.8 us -> 57.5 us (1.012)
  Pallas kernels: 55.1 us -> 55.8 us
    pallas_call x1, Pallas kernels: 55.1 us -> 55.8 us  [on_device(): pl.pallas_call(functools.partial(kernel, rows, cols), out_shape=jax.Shape...]
where the time goes in v4:
time: 57.5 us; the launch traced here: 57.3 us
  Pallas kernels  55.8 us (97%)
  local copies, waits for them, and re-layouts  1.54 us (3%)
    pallas_call x1, Pallas kernels, on_device(): pl.pallas_call(functools.partial(kernel, rows, cols), out_shape=jax.Shape...  55.8 us
    unnamed x1, local copies, waits for them, and re-layouts  1.54 us

profile of v4, /device:TPU:1, one launch (start us, length us, event | category | flops | bytes accessed | tf_op | source)
XLA Modules:
  0.0 57.3 jit_solution(5179362044854538877)
XLA Ops:
  0.0 55.8 %shard_map.55 = bf16[12,3072]{1,0:T(8,128)(2,1)} custom-call(bf16[12,3072]{1,0:T(8,128)(2,1)} %tok_ref.1, bf16[3072,6144]{1,0:T(8,128)(2,1)} %up_ref.1, f32[1,6144]{1,0:T(1,128)} %bitcast.2, bf16[6144,3072]{1,0:T(8,128)(2,1)} %down_ref.1, f32[1,3072]{1,0:T(1,128)} %bitcast.3), custom_call_target="tpu_custom_call" | custom-call | flops 7247757312 | bytes 75497472 | tf_op jit(solution)/shard_map/pallas_call | solution.py:267
  55.8 1.5 %copy.7 = bf16[12,3072]{1,0:T(8,128)(2,1)} copy(bf16[12,3072]{1,0:T(8,128)(2,1)} %shard_map.55) | data formatting | bytes 147456

commit v5 on v4

--- a/solution.py
+++ b/solution.py
@@ -7,7 +7,7 @@
 from jax.experimental.pallas import tpu as pltpu
 from jax.sharding import PartitionSpec as P
 
-PIECE = 256
+PIECE = 128
 SPLIT = 4
 MESH = pl.DeviceIdType.MESH
 
@@ -74,7 +74,7 @@
     def _():
         greet(outer, c)
 
-    early = min(3, u_slots)
+    early = min(6, u_slots)
     each(0, early, lambda j: load_up(j).start())
 
     mine = tok_ref[...].astype(jnp.float32)
@@ -128,9 +128,9 @@
             send_sem=out_send.at[i], recv_sem=c_recv.at[i],
             device_id=(outer, c), device_id_type=MESH)
 
-    lag_in = 1 + 2 * (half - 1 - depth)
-    lag_out = 2 * half + 1 + 3 * depth
-    ticks = n + 2 * half + 1 + 3 * (half - 1)
+    lag_in = 1 + 4 * (half - 1 - depth)
+    lag_out = 4 * half + 6 * depth
+    ticks = n + 4 * half + 6 * (half - 1)
 
     def tick(t):
         a = t - lag_in

time: 57.5 us -> 57.4 us (level)
  no operation moved by 1% of the time
where the time goes in v5:
time: 57.4 us; the launch traced here: 57.2 us
  Pallas kernels  55.7 us (97%)
  local copies, waits for them, and re-layouts  1.54 us (3%)
    pallas_call x1, Pallas kernels, on_device(): pl.pallas_call(functools.partial(kernel, rows, cols), out_shape=jax.Shape...  55.7 us
    unnamed x1, local copies, waits for them, and re-layouts  1.54 us

profile of v5, /device:TPU:1, one launch (start us, length us, event | category | flops | bytes accessed | tf_op | source)
XLA Modules:
  0.0 57.2 jit_solution(7319379225570291893)
XLA Ops:
  0.0 55.7 %shard_map.55 = bf16[12,3072]{1,0:T(8,128)(2,1)} custom-call(bf16[12,3072]{1,0:T(8,128)(2,1)} %tok_ref.1, bf16[3072,6144]{1,0:T(8,128)(2,1)} %up_ref.1, f32[1,6144]{1,0:T(1,128)} %bitcast.2, bf16[6144,3072]{1,0:T(8,128)(2,1)} %down_ref.1, f32[1,3072]{1,0:T(1,128)} %bitcast.3), custom_call_target="tpu_custom_call" | custom-call | flops 7247757312 | bytes 75497472 | tf_op jit(solution)/shard_map/pallas_call | solution.py:267
  55.7 1.5 %copy.7 = bf16[12,3072]{1,0:T(8,128)(2,1)} copy(bf16[12,3072]{1,0:T(8,128)(2,1)} %shard_map.55) | data formatting | bytes 147456
